TPU v7x, 128 devices: a whole 4x4x4 slice. The times are simulated.
128 devices in a mesh: prefix: 8 (over z, core), seq: 16 (over x, y).
Axes of the slice: x: 4, y: 4, z: 4, core: 2. Of those that a mesh axis runs over, the one named last changes fastest.
Arguments:
- queries: bfloat16 [1024, 4, 8192], P(('prefix', 'seq')), may hold values from -28 to 28
- new_keys: bfloat16 [1024, 4, 1024], P(('prefix', 'seq')), may hold values from -24 to 24
- new_values: bfloat16 [1024, 4, 1024], P(('prefix', 'seq')), may hold values from -6 to 6
- suffix_keys: bfloat16 [1024, 256, 1024], P(('prefix', 'seq')), may hold values from -24 to 24
- suffix_values: bfloat16 [1024, 256, 1024], P(('prefix', 'seq')), may hold values from -6 to 6
- suffix_len: int32 [1024], P(('prefix', 'seq')), may hold values from 1 to 256, 131072 in all
- row_prefix: int32 [1024, 1], P(('prefix', 'seq')), may hold values from 0 to 7; in each aligned block of 8 rows (0 to 7, 8 to 15, ...) at most 2 rows name the same one
- prefix_key_codes: bfloat16 [8, 12288, 1024], P('prefix', 'seq'), may hold values from -48 to 48
- prefix_value_codes: bfloat16 [8, 12288, 1024], P('prefix', 'seq'), may hold values from -6 to 6
- scale_index: int32 [8, 96, 8], P('prefix', 'seq'), may hold values from 0 to 255
- scale_table: float32 [2, 256], replicated, may hold values from 0.5 to 2, as said below
Outputs:
- attended: bfloat16 [1024, 4, 8192], P(('prefix', 'seq'))
Inputs may be any that keep to these rules, and one draw needn't show every extreme that they name: `row_prefix`: among the rows of one device, at most 2 name any one prefix, a bound that some block reaches of them. `scale_table`: every entry is 0.5, 1 or 2.
All inputs are finite; a program needn't handle non-finite values. No bound on the sum of `suffix_len` on one device may be relied on, other than what follows from the above.
Results may differ from a plain program's by a relative error of at most 0.0046.
Values may be sent and summed in bfloat16 or wider, within the bound.
No kernel may reach another device: no remote copies, remote signals or barrier semaphores. Data moves between devices by JAX's collectives and lax.ppermute only.
A program may use at most 256 MiB of HBM per device.

v0:
```python
import functools
import math

import jax
import jax.numpy as jnp
from jax import lax
from jax.experimental import pallas as pl
from jax.experimental.pallas import tpu as pltpu
from jax.sharding import PartitionSpec as P

QH = 64
KVH = 8
HD = 128
STEPS = 4
BLOCK = 128
GROUP = QH // KVH
QROWS = GROUP * STEPS
SLOTS = 2
PASSES = 2
PIECES = 2
TQ = 256
EXTRA = 8
SCALE = HD**-0.5
SCALE2 = SCALE * math.log2(math.e)
LN2 = math.log(2.0)
FLOOR = -1e30
NT = (((1,), (1,)), ((), ()))
MIB = 2**20


def arrange(rows):
    wide = rows.astype(jnp.float32)
    heads = []
    for k in range(KVH):
        parts = [wide[:, (k * GROUP + g) * HD : (k * GROUP + g + 1) * HD] for g in range(GROUP)]
        heads.append(jnp.concatenate(parts, axis=0))
    return heads


def slot_of_row(names, row, rows):
    prefix = names[row]
    seen = jnp.int32(0)
    for r in range(rows):
        earlier = jnp.logical_and(names[r] == prefix, r < row)
        seen = seen + earlier.astype(jnp.int32)
    return prefix, seen


def slot_index(prefix, slot):
    return (prefix // 2) * (2 * SLOTS) + slot * 2 + prefix % 2


def outgoing_kernel(names, q_ref, o_ref, a_ref):
    rows = q_ref.shape[0]
    o_ref[...] = jnp.zeros_like(o_ref)
    for r in range(rows):
        prefix, slot = slot_of_row(names, r, rows)
        place = slot_index(prefix, slot)
        heads = arrange(q_ref[r])
        for k in range(KVH):
            head = heads[k].astype(jnp.bfloat16)
            o_ref[place, k] = head
            a_ref[r, k] = head


def outgoing_queries(names, queries):
    slots = 8 * SLOTS
    return pl.pallas_call(
        outgoing_kernel,
        in_specs=[
            pl.BlockSpec(memory_space=pltpu.SMEM),
            pl.BlockSpec(memory_space=pltpu.VMEM),
        ],
        out_specs=[pl.BlockSpec(memory_space=pltpu.VMEM)] * 2,
        out_shape=[
            jax.ShapeDtypeStruct((slots, KVH, QROWS, HD), jnp.bfloat16),
            jax.ShapeDtypeStruct((queries.shape[0], KVH, QROWS, HD), jnp.bfloat16),
        ],
        cost_estimate=pl.CostEstimate(flops=0, bytes_accessed=2 * MIB, transcendentals=0),
    )(names, queries)


def prepare_kernel(core_ref, index_ref, table_ref, k_ref, v_ref, keep_ref, send_ref):
    head = pl.program_id(0)
    core = core_ref[0]
    blocks = keep_ref.shape[2] // BLOCK
    for kind, ref in enumerate((k_ref, v_ref)):
        for side, out_ref in ((core, keep_ref), (1 - core, send_ref)):
            for i in range(blocks):
                b = side * blocks + i
                scale = table_ref[kind, index_ref[b, head]]
                codes = ref[0, pl.ds(pl.multiple_of(b * BLOCK, BLOCK), BLOCK), :]
                scaled = codes.astype(jnp.float32) * scale
                if kind == 1:
                    scaled = scaled.T
                out_ref[0, kind, pl.ds(i * BLOCK, BLOCK)] = scaled.astype(jnp.bfloat16)


def prepare(core, index, table, key_codes, value_codes):
    tokens = key_codes.shape[1]
    half = tokens // 2
    smem = pl.BlockSpec(memory_space=pltpu.SMEM)
    codes = pl.BlockSpec((1, tokens, HD), lambda k, core: (0, 0, k))
    block = (1, 2, half, HD)
    return pl.pallas_call(
        prepare_kernel,
        grid_spec=pltpu.PrefetchScalarGridSpec(
            num_scalar_prefetch=1,
            grid=(KVH,),
            in_specs=[smem, smem, codes, codes],
            out_specs=[
                pl.BlockSpec(block, lambda k, core: (core[0] * KVH + k, 0, 0, 0)),
                pl.BlockSpec(block, lambda k, core: (k, 0, 0, 0)),
            ],
        ),
        out_shape=[
            jax.ShapeDtypeStruct((2 * KVH, 2, half, HD), jnp.bfloat16),
            jax.ShapeDtypeStruct((KVH, 2, half, HD), jnp.bfloat16),
        ],
        cost_estimate=pl.CostEstimate(flops=0, bytes_accessed=MIB // 8, transcendentals=0),
    )(core, index, table, key_codes, value_codes)


def attend_kernel(first, last, *refs):
    refs = list(refs)
    q_ref, kv_ref = refs[:2]
    refs = refs[2:]
    before_ref = None if first else refs.pop(0)
    if last:
        out_ref = refs.pop(0)
        sa, sb, ma, mb, mid_ref = refs
    else:
        mid_ref, sa, sb, ma, mb = refs
    total = q_ref.shape[0]
    tiles = total // TQ
    sources, _, part, _ = kv_ref.shape
    run = sources // PASSES
    span = run * part

    def finish(turn, tile, both, top):
        columns = pl.ds(pl.multiple_of(tile * TQ, TQ), TQ)
        acc, sums = both[:HD], both[HD : HD + 8]
        if turn > 0 or not first:
            old_ref = mid_ref if turn > 0 else before_ref
            old_top = old_ref[HD + 8 :, columns]
            joint = jnp.maximum(old_top, top)
            old, new = jnp.exp2(old_top - joint), jnp.exp2(top - joint)
            acc = acc * new[:1] + old_ref[:HD, columns] * old[:1]
            sums = sums * new + old_ref[HD : HD + 8, columns] * old
            top = joint
        if turn < PASSES - 1 or not last:
            mid_ref[:HD, columns] = acc
            mid_ref[HD : HD + 8, columns] = sums
            mid_ref[HD + 8 :, columns] = top
            return
        out = (acc * (1.0 / sums[:1])).T.astype(jnp.bfloat16)
        lse = (top + jnp.log2(sums)) * LN2
        high = lse.astype(jnp.bfloat16).astype(jnp.float32)
        middle = (lse - high).astype(jnp.bfloat16).astype(jnp.float32)
        low = lse - high - middle
        line = lax.broadcasted_iota(jnp.int32, (EXTRA, TQ), 0)
        parts = jnp.where(line == 0, high, jnp.where(line == 1, middle, low)).astype(jnp.bfloat16)
        slots = TQ // QROWS
        out_ref[pl.ds(tile * slots, slots), :QROWS] = out.reshape(slots, QROWS, HD)
        for n in range(slots):
            lanes = n * QROWS // HD * HD
            out_ref[tile * slots + n, QROWS:] = parts[:, lanes : lanes + HD]

    def stage(score, weigh, s1, m1, s2, m2):
        if weigh:
            top = jnp.broadcast_to(jnp.max(m2[...], axis=0, keepdims=True) * SCALE2, (8, TQ))
        if score:
            q = q_ref[pl.ds(pl.multiple_of(score[1] * TQ, TQ), TQ), :]
            best = None
        both = None
        step = run // PIECES
        piece = step * part
        for n in range(PIECES):
            tokens = pl.ds(n * piece, piece)
            if score:
                keys = kv_ref[pl.ds(score[0] * run + n * step, step), 0].reshape(piece, HD)
                s = lax.dot_general(keys, q, NT, preferred_element_type=jnp.float32)
                s1[tokens, :] = s
                high = jnp.max(s.reshape(piece // 8, 8, TQ), axis=0)
                best = high if best is None else jnp.maximum(best, high)
            if weigh:
                weights = jnp.exp2(s2[tokens, :] * SCALE2 - top[:1]).astype(jnp.bfloat16)
                values = [
                    kv_ref[weigh[0] * run + n * step + j, 1, pl.ds(i * BLOCK, BLOCK), :]
                    for j in range(step)
                    for i in range(part // BLOCK)
                ]
                values = jnp.concatenate(values, axis=1)
                values = jnp.concatenate([values, jnp.ones((16, piece), jnp.bfloat16)], axis=0)
                more = jnp.dot(values, weights, preferred_element_type=jnp.float32)
                both = more if both is None else both + more
        if score:
            m1[...] = best
        if weigh:
            finish(weigh[0], weigh[1], both, top)

    stage((0, 0), None, sa, ma, sb, mb)
    for turn in range(PASSES):

        def double(g, carry):
            stage((turn, 2 * g + 1), (turn, 2 * g), sb, mb, sa, ma)
            stage((turn, 2 * g + 2), (turn, 2 * g + 1), sa, ma, sb, mb)
            return carry

        lax.fori_loop(0, tiles // 2 - 1, double, 0)
        stage((turn, tiles - 1), (turn, tiles - 2), sb, mb, sa, ma)
        following = (turn + 1, 0) if turn + 1 < PASSES else None
        stage(following, (turn, tiles - 1), sa, ma, sb, mb)


def attend(first, last, q, kv, state):
    total = q.shape[0]
    vmem = pl.BlockSpec(memory_space=pltpu.VMEM)
    tokens = kv.shape[0] * kv.shape[2]
    scratch = [pltpu.VMEM((tokens // PASSES, TQ), jnp.float32)] * 2
    scratch += [pltpu.VMEM((8, TQ), jnp.float32)] * 2
    held = (HD + 16, total)
    if last:
        shape = jax.ShapeDtypeStruct((total // QROWS, QROWS + EXTRA, HD), jnp.bfloat16)
        scratch.append(pltpu.VMEM(held, jnp.float32))
    else:
        shape = jax.ShapeDtypeStruct(held, jnp.float32)
    return pl.pallas_call(
        functools.partial(attend_kernel, first, last),
        in_specs=[vmem] * (2 + len(state)),
        out_specs=vmem,
        out_shape=shape,
        scratch_shapes=scratch,
        compiler_params=pltpu.CompilerParams(vmem_limit_bytes=40 * MIB),
        cost_estimate=pl.CostEstimate(
            flops=8 * total * tokens * HD, bytes_accessed=4 * MIB, transcendentals=total * tokens
        ),
    )(q, kv, *state)


def local_kernel(lens, q_ref, nk_ref, nv_ref, sk_ref, sv_ref, o_ref, l_ref):
    length = lens[pl.program_id(0)]
    suffix = sk_ref.shape[1]
    new_keys = nk_ref[0].astype(jnp.float32)
    new_values = nv_ref[0].astype(jnp.float32)
    pad = jnp.zeros((GROUP * 2 - STEPS, HD), jnp.float32)
    visible = lax.broadcasted_iota(jnp.int32, (QROWS, suffix), 1) < length
    step = lax.broadcasted_iota(jnp.int32, (QROWS, 2 * GROUP), 0) % STEPS
    fresh = lax.broadcasted_iota(jnp.int32, (QROWS, 2 * GROUP), 1) <= step
    for k in range(KVH):
        lanes = slice(k * HD, (k + 1) * HD)
        q = q_ref[0, k]
        nk = jnp.concatenate([new_keys[:, lanes], pad], axis=0).astype(jnp.bfloat16)
        nv = jnp.concatenate([new_values[:, lanes], pad], axis=0).astype(jnp.bfloat16)
        s = lax.dot_general(q, sk_ref[0, :, lanes], NT, preferred_element_type=jnp.float32)
        n = lax.dot_general(q, nk, NT, preferred_element_type=jnp.float32)
        s = jnp.where(visible, s * SCALE, FLOOR)
        n = jnp.where(fresh, n * SCALE, FLOOR)
        top = jnp.maximum(jnp.max(s, axis=1, keepdims=True), jnp.max(n, axis=1, keepdims=True))
        es, en = jnp.exp(s - top), jnp.exp(n - top)
        sums = jnp.sum(es, axis=1, keepdims=True) + jnp.sum(en, axis=1, keepdims=True)
        out = jnp.dot(
            es.astype(jnp.bfloat16), sv_ref[0, :, lanes], preferred_element_type=jnp.float32
        ) + jnp.dot(en.astype(jnp.bfloat16), nv, preferred_element_type=jnp.float32)
        o_ref[0, k] = out / sums
        l_ref[0, k] = jnp.broadcast_to(top + jnp.log(sums), (QROWS, HD))


def local_attention(lens, queries, new_keys, new_values, suffix_keys, suffix_values):
    rows, suffix, width = suffix_keys.shape

    def by_row(*shape):
        return pl.BlockSpec((1,) + shape, lambda r, lens: (r,) + (0,) * len(shape))

    return pl.pallas_call(
        local_kernel,
        grid_spec=pltpu.PrefetchScalarGridSpec(
            num_scalar_prefetch=1,
            grid=(rows,),
            in_specs=[
                by_row(KVH, QROWS, HD),
                by_row(STEPS, width),
                by_row(STEPS, width),
                by_row(suffix, width),
                by_row(suffix, width),
            ],
            out_specs=[by_row(KVH, QROWS, HD)] * 2,
        ),
        out_shape=[jax.ShapeDtypeStruct((rows, KVH, QROWS, HD), jnp.float32)] * 2,
        compiler_params=pltpu.CompilerParams(vmem_limit_bytes=24 * MIB),
        cost_estimate=pl.CostEstimate(
            flops=4 * rows * QH * STEPS * suffix * HD,
            bytes_accessed=10 * MIB,
            transcendentals=rows * QH * STEPS * suffix,
        ),
    )(lens, queries, new_keys, new_values, in_hbm(suffix_keys), in_hbm(suffix_values))


def combine_kernel(names, first_lane, back_ref, out_ref, lse_ref, o_ref):
    rows = out_ref.shape[0]
    lane = lax.broadcasted_iota(jnp.int32, (QROWS, HD), 1)
    row = lax.broadcasted_iota(jnp.int32, (QROWS, HD), 0)
    mine = lane == row + first_lane[0]

    def mix(r, carry):
        prefix, slot = slot_of_row(names, r, rows)
        place = slot_index(prefix, slot)
        for k in range(KVH):
            prefix_out = back_ref[place, k, :QROWS].astype(jnp.float32)
            parts = back_ref[place, k, QROWS:].astype(jnp.float32)
            spread = jnp.where(mine, parts[:1] + parts[1:2] + parts[2:3], 0.0)
            prefix_lse = jnp.sum(spread, axis=1, keepdims=True)
            local_lse = lse_ref[r, k]
            joint = jnp.maximum(local_lse, prefix_lse)
            local_share = jnp.exp(local_lse - joint)
            prefix_share = jnp.exp(prefix_lse - joint)
            mixed = (local_share * out_ref[r, k] + prefix_share * prefix_out) / (
                local_share + prefix_share
            )
            for g in range(GROUP):
                o_ref[r, :, (k * GROUP + g) * HD : (k * GROUP + g + 1) * HD] = mixed[
                    g * STEPS : (g + 1) * STEPS
                ].astype(jnp.bfloat16)
        return carry

    lax.fori_loop(0, rows, mix, 0)


def in_hbm(x):
    return pltpu.with_memory_space_constraint(x, pltpu.HBM)


def combine(names, first_lane, back, local_out, local_lse):
    rows = local_out.shape[0]
    vmem = pl.BlockSpec(memory_space=pltpu.VMEM)
    return pl.pallas_call(
        combine_kernel,
        in_specs=[pl.BlockSpec(memory_space=pltpu.SMEM)] * 2 + [vmem] * 3,
        out_specs=vmem,
        out_shape=jax.ShapeDtypeStruct((rows, STEPS, QH * HD), jnp.bfloat16),
        cost_estimate=pl.CostEstimate(flops=0, bytes_accessed=4 * MIB, transcendentals=0),
    )(names, first_lane, in_hbm(back), in_hbm(local_out), in_hbm(local_lse))


def local(
    queries,
    new_keys,
    new_values,
    suffix_keys,
    suffix_values,
    suffix_len,
    row_prefix,
    prefix_key_codes,
    prefix_value_codes,
    scale_index,
    scale_table,
):
    groups = lax.axis_size("prefix")
    shards = lax.axis_size("seq")
    core = lax.axis_index("prefix") % 2
    swap = [(i, i ^ 1) for i in range(groups)]
    names = row_prefix[:, 0]

    outgoing, arranged = outgoing_queries(names, queries)
    outgoing, key_codes, value_codes = lax.optimization_barrier(
        (outgoing, prefix_key_codes, prefix_value_codes)
    )
    arrived = lax.all_to_all(
        outgoing.reshape(groups * shards, QROWS, HD),
        ("prefix", "seq"),
        split_axis=0,
        concat_axis=0,
        tiled=True,
    )
    keep, send = prepare(
        core.reshape(1).astype(jnp.int32), scale_index[0], scale_table, key_codes, value_codes
    )
    received = lax.ppermute(send, "prefix", swap)
    q = arrived.reshape(-1, HD)
    moved = lax.dynamic_update_slice(keep, received, ((1 - core) * KVH, 0, 0, 0))
    moved, q = lax.optimization_barrier((moved, q))
    own = lax.all_to_all(moved, "seq", split_axis=0, concat_axis=0, tiled=True)
    other = lax.ppermute(own, "prefix", swap)
    state = attend(True, False, q, own, ())
    answer = attend(False, True, q, other, (state,))
    local_out, local_lse = local_attention(
        suffix_len, arranged, new_keys, new_values, suffix_keys, suffix_values
    )
    back = lax.all_to_all(answer, ("prefix", "seq"), split_axis=0, concat_axis=0, tiled=True)
    back = back.reshape(groups * SLOTS, KVH, QROWS + EXTRA, HD)
    first_lane = lax.axis_index("seq") % (HD // QROWS) * QROWS
    return combine(names, first_lane.reshape(1).astype(jnp.int32), back, local_out, local_lse)


def solution(mesh):
    return jax.shard_map(
        local,
        mesh=mesh,
        in_specs=(
            P(("prefix", "seq"), None, None),
            P(("prefix", "seq"), None, None),
            P(("prefix", "seq"), None, None),
            P(("prefix", "seq"), None, None),
            P(("prefix", "seq"), None, None),
            P(("prefix", "seq")),
            P(("prefix", "seq"), None),
            P("prefix", "seq", None),
            P("prefix", "seq", None),
            P("prefix", "seq", None),
            P(),
        ),
        out_specs=P(("prefix", "seq"), None, None),
        check_vma=False,
    )
```

profile of v0, /device:TPU:0, one launch (start us, length us, event | category | flops | bytes accessed | tf_op | source)
XLA Modules:
  0.0 167.8 jit_solution(12424531285875346816)
XLA Ops:
  0.0 1.3 copy.14
  1.3 2.5 %shard_map.109 = (bf16[16,8,32,128]{3,2,1,0:T(8,128)(2,1)}, bf16[8,8,32,128]{3,2,1,0:T(8,128)(2,1)}) custom-call(s32[8]{0:T(128)} %bitcast.14, bf16[8,4,8192]{2,1,0:T(4,128)(2,1)} %q_ref.1), custom_call_target="tpu_custom_call" | custom-call | bytes 2097152 | tf_op jit(solution)/shard_map/pallas_call | solution.py:68
  3.8 6.9 %shard_map.110 = (bf16[16,2,384,128]{3,2,1,0:T(8,128)(2,1)}, bf16[8,2,384,128]{3,2,1,0:T(8,128)(2,1)}) custom-call(s32[1]{0:T(128)} %bitcast.2.core_ref, s32[6,8]{1,0:T(8,128)} %bitcast.13, f32[2,256]{1,0:T(2,128)} %table_ref.1, bf16[1,768,1024]{2,1,0:T(8,128)(2,1)} %k_ref, bf16[1,768,1024]{2,1,0:T(8,128)(2,1)} %v_ref), custom_call_target="tpu_custom_call" | custom-call | bytes 131072 | tf_op jit(solution)/shard_map/pallas_call | solution.py:105
  10.7 0.0 collective-permute-start
  10.7 11.3 %all-to-all-start = ((bf16[128,32,128]{2,1,0:T(8,128)(2,1)}), bf16[128,32,128]{2,1,0:T(8,128)(2,1)S(1)}, u32[]{:S(2)}, u32[]{:S(2)}) async-start(bf16[128,32,128]{2,1,0:T(8,128)(2,1)} %bitcast.12), calls=%async_computation | async-start | bytes 2097152 | tf_op jit(solution)/shard_map/all_to_all | solution.py:368
  21.9 0.0 collective-permute-done
  21.9 1.3 constant_dynamic-update-slice_fusion
  23.2 17.8 %all-to-all-done = bf16[128,32,128]{2,1,0:T(8,128)(2,1)S(1)} async-done(((bf16[128,32,128]{2,1,0:T(8,128)(2,1)}), bf16[128,32,128]{2,1,0:T(8,128)(2,1)S(1)}, u32[]{:S(2)}, u32[]{:S(2)}) %all-to-all-start) | async-done | bytes 1048608 | tf_op jit(solution)/shard_map/all_to_all | solution.py:368
  41.0 42.7 %all_to_all.15.refs_1_ = bf16[16,2,384,128]{3,2,1,0:T(8,128)(2,1)S(1)} all-to-all(bf16[16,2,384,128]{3,2,1,0:T(8,128)(2,1)} %constant_dynamic-update-slice_fusion), channel_id=1, replica_groups=mesh['prefix'=8,'seq'=16] {'seq'}, dimensions={0} | all-to-all | bytes 6291456 | tf_op jit(solution)/shard_map/all_to_all | solution.py:382
  83.7 0.0 collective-permute-start.1
  83.7 24.5 %shard_map.111.refs_2_ = f32[144,4096]{1,0:T(8,128)S(1)} custom-call(bf16[4096,128]{1,0:T(8,128)(2,1)S(1)} %bitcast.9, bf16[16,2,384,128]{3,2,1,0:T(8,128)(2,1)S(1)} %all_to_all.15.refs_1_), custom_call_target="tpu_custom_call" | custom-call | flops 25769803776 | bytes 4194304 | tf_op jit(solution)/shard_map/pallas_call | solution.py:228
  108.2 0.0 copy-start.2
  108.2 0.0 copy-start.3
  108.2 0.0 copy-start.4
  108.2 0.0 copy-start.5
  108.2 0.0 collective-permute-done.1.refs_1_
  108.2 27.1 %shard_map.112 = bf16[128,40,128]{2,1,0:T(8,128)(2,1)} custom-call(bf16[4096,128]{1,0:T(8,128)(2,1)S(1)} %bitcast.10, bf16[16,2,384,128]{3,2,1,0:T(8,128)(2,1)S(1)} %collective-permute-done.1.refs_1_, f32[144,4096]{1,0:T(8,128)S(1)} %shard_map.111.refs_2_), custom_call_target="tpu_custom_call" | custom-call | flops 25769803776 | bytes 4194304 | tf_op jit(solution)/shard_map/pallas_call | solution.py:228
  135.3 5.4 %all-to-all-start.2 = ((bf16[128,40,128]{2,1,0:T(8,128)(2,1)}), bf16[128,40,128]{2,1,0:T(8,128)(2,1)S(1)}, u32[]{:S(2)}, u32[]{:S(2)}) async-start(bf16[128,40,128]{2,1,0:T(8,128)(2,1)} %shard_map.112), calls=%async_computation.2 | async-start | bytes 2621440 | tf_op jit(solution)/shard_map/all_to_all | solution.py:389
  140.8 0.0 copy-done.2
  140.8 0.0 copy-done.3
  140.8 0.0 copy-done.4
  140.8 0.0 copy-done.5
  140.8 19.4 %shard_map.113 = (f32[8,8,32,128]{3,2,1,0:T(8,128)S(1)}, f32[8,8,32,128]{3,2,1,0:T(8,128)S(1)}) custom-call(s32[8]{0:T(128)S(1)} %copy-done.5, bf16[8,8,32,128]{3,2,1,0:T(8,128)(2,1)S(1)} %copy-done.2, bf16[8,4,1024]{2,1,0:T(4,128)(2,1)S(1)} %copy-done.3, bf16[8,4,1024]{2,1,0:T(4,128)(2,1)S(1)} %copy-done.4, bf16[8,256,1024]{2,1,0:T(8,128)(2,1)} %sk_ref.1, ...), custom_call_target="tpu_custom_call" | custom-call | flops 268435456 | bytes 10485760 | tf_op jit(solution)/shard_map/pallas_call | solution.py:275
  160.2 0.0 copy-start
  160.2 1.0 copy-done
  161.1 0.0 copy-start.1
  161.1 1.0 copy-done.1
  162.1 0.4 all-to-all-done.2
  162.5 0.0 copy-start.6
  162.5 1.1 copy-done.6
  163.6 4.2 %shard_map.114 = bf16[8,4,8192]{2,1,0:T(4,128)(2,1)} custom-call(s32[8]{0:T(128)} %bitcast.15, s32[1]{0:T(128)} %bitcast.1.first_lane, bf16[16,8,40,128]{3,2,1,0:T(8,128)(2,1)} %bitcast.11, f32[8,8,32,128]{3,2,1,0:T(8,128)} %copy-done, f32[8,8,32,128]{3,2,1,0:T(8,128)} %copy-done.1), custom_call_target="tpu_custom_call" | custom-call | bytes 4194304 | tf_op jit(solution)/shard_map/pallas_call | solution.py:336
Async XLA Ops:
  10.7 11.3 %collective-permute-start = (bf16[8,2,384,128]{3,2,1,0:T(8,128)(2,1)}, bf16[8,2,384,128]{3,2,1,0:T(8,128)(2,1)S(1)}, u32[]{:S(2)}, u32[]{:S(2)}) collective-permute-start(bf16[8,2,384,128]{3,2,1,0:T(8,128)(2,1)} %get-tuple-element.20), channel_id=1, source_target_pairs={{0,16},{16,0},{32,48},{48,32},{64,80},{80,64},{96,112},{112,96},{1... | collective-permute-start | bytes 4718600 | tf_op jit(solution)/shard_map/ppermute | solution.py:378
  10.7 30.3 %all-to-all-start = ((bf16[128,32,128]{2,1,0:T(8,128)(2,1)}), bf16[128,32,128]{2,1,0:T(8,128)(2,1)S(1)}, u32[]{:S(2)}, u32[]{:S(2)}) async-start(bf16[128,32,128]{2,1,0:T(8,128)(2,1)} %bitcast.12), calls=%async_computation | async-start | bytes 2097152 | tf_op jit(solution)/shard_map/all_to_all | solution.py:368
  83.7 24.5 %collective-permute-start.1 = (bf16[16,2,384,128]{3,2,1,0:T(8,128)(2,1)S(1)}, bf16[16,2,384,128]{3,2,1,0:T(8,128)(2,1)S(1)}, u32[]{:S(2)}, u32[]{:S(2)}) collective-permute-start(bf16[16,2,384,128]{3,2,1,0:T(8,128)(2,1)S(1)} %all_to_all.15.refs_1_), channel_id=1, source_target_pairs={{0,16},{16,0},{32,48},{48,32},{64,80},{80,64},{96,112},{112,96},{1... | collective-permute-start | bytes 9437192 | tf_op jit(solution)/shard_map/ppermute | solution.py:383
  108.2 32.6 %copy-start.2 = (bf16[8,8,32,128]{3,2,1,0:T(8,128)(2,1)S(1)}, bf16[8,8,32,128]{3,2,1,0:T(8,128)(2,1)}, u32[]{:S(2)}) copy-start(bf16[8,8,32,128]{3,2,1,0:T(8,128)(2,1)} %get-tuple-element.24.q_ref) | copy-start | bytes 1572868
  108.2 32.6 %copy-start.3 = (bf16[8,4,1024]{2,1,0:T(4,128)(2,1)S(1)}, bf16[8,4,1024]{2,1,0:T(4,128)(2,1)}, u32[]{:S(2)}) copy-start(bf16[8,4,1024]{2,1,0:T(4,128)(2,1)} %nk_ref.1) | copy-start | bytes 196612
  108.2 32.6 %copy-start.4 = (bf16[8,4,1024]{2,1,0:T(4,128)(2,1)S(1)}, bf16[8,4,1024]{2,1,0:T(4,128)(2,1)}, u32[]{:S(2)}) copy-start(bf16[8,4,1024]{2,1,0:T(4,128)(2,1)} %nv_ref.1) | copy-start | bytes 196612
  108.2 32.6 %copy-start.5 = (s32[8]{0:T(128)S(1)}, s32[8]{0:T(128)}, u32[]{:S(2)}) copy-start(s32[8]{0:T(128)} %lens.1) | copy-start | bytes 100
  135.3 27.2 %all-to-all-start.2 = ((bf16[128,40,128]{2,1,0:T(8,128)(2,1)}), bf16[128,40,128]{2,1,0:T(8,128)(2,1)S(1)}, u32[]{:S(2)}, u32[]{:S(2)}) async-start(bf16[128,40,128]{2,1,0:T(8,128)(2,1)} %shard_map.112), calls=%async_computation.2 | async-start | bytes 2621440 | tf_op jit(solution)/shard_map/all_to_all | solution.py:389
  160.2 1.0 copy-start
  161.1 1.0 copy-start.1
  162.5 1.1 copy-start.6
where the time goes:
time: 168 us
  Pallas kernels  84.5 us (50%)
  blocking collectives  42.7 us (25%)
  waiting for transfers between devices  18.2 us (11%)
  starting transfers between devices  16.7 us (10%)
  local copies, waits for them, and re-layouts  5.57 us (3%)
    pallas_call x2, Pallas kernels, attend(): pl.pallas_call(functools.partial(attend_kernel, first, last), in_specs=[v...  51.6 us
    all_to_all x1, blocking collectives, local(): own = lax.all_to_all(moved, 'seq', split_axis=0, concat_axis=0, tiled=True)  42.7 us
    pallas_call x1, Pallas kernels, local_attention(): pl.pallas_call(local_kernel, grid_spec=pltpu.PrefetchScalarGridSpec(num_s...  19.4 us
    all_to_all x1, waiting for transfers between devices, local(): lax.all_to_all(outgoing.reshape(groups * shards, QROWS, HD), ('prefix', '...  17.8 us
    all_to_all x1, starting transfers between devices, local(): lax.all_to_all(outgoing.reshape(groups * shards, QROWS, HD), ('prefix', '...  11.3 us
    pallas_call x1, Pallas kernels, prepare(): pl.pallas_call(prepare_kernel, grid_spec=pltpu.PrefetchScalarGridSpec(num...  6.86 us
    all_to_all x1, starting transfers between devices, local(): lax.all_to_all(answer, ('prefix', 'seq'), split_axis=0, concat_axis=0, ti...  5.39 us
    unnamed x15, local copies, waits for them, and re-layouts  4.32 us
  transfers between devices with their start and end apart: 4, of which 2 were waited for; matrix products, arithmetic and copies ran while one was open for 1% of the time, Pallas kernels for 26%

commit v1 on v0

--- a/solution.py
+++ b/solution.py
@@ -80,45 +80,43 @@
     )(names, queries)
 
 
-def prepare_kernel(core_ref, index_ref, table_ref, k_ref, v_ref, keep_ref, send_ref):
+def prepare_kernel(core_ref, mine_ref, other_ref, table_ref, k_ref, v_ref, got_ref, o_ref):
     head = pl.program_id(0)
     core = core_ref[0]
-    blocks = keep_ref.shape[2] // BLOCK
-    for kind, ref in enumerate((k_ref, v_ref)):
-        for side, out_ref in ((core, keep_ref), (1 - core, send_ref)):
+    blocks = o_ref.shape[3] // BLOCK
+    for source in range(2):
+        place = core if source == 0 else 1 - core
+        index_ref = mine_ref if source == 0 else other_ref
+        for kind in range(2):
             for i in range(blocks):
-                b = side * blocks + i
-                scale = table_ref[kind, index_ref[b, head]]
-                codes = ref[0, pl.ds(pl.multiple_of(b * BLOCK, BLOCK), BLOCK), :]
+                tokens = pl.ds(i * BLOCK, BLOCK)
+                scale = table_ref[kind, index_ref[core * blocks + i, head]]
+                if source == 0:
+                    codes = (k_ref, v_ref)[kind][0, tokens, :]
+                else:
+                    codes = got_ref[kind, tokens, :]
                 scaled = codes.astype(jnp.float32) * scale
                 if kind == 1:
                     scaled = scaled.T
-                out_ref[0, kind, pl.ds(i * BLOCK, BLOCK)] = scaled.astype(jnp.bfloat16)
-
-
-def prepare(core, index, table, key_codes, value_codes):
-    tokens = key_codes.shape[1]
-    half = tokens // 2
+                o_ref[place, 0, kind, tokens] = scaled.astype(jnp.bfloat16)
+
+
+def prepare(core, index, other_index, table, key_codes, value_codes, received):
+    half = key_codes.shape[1] // 2
     smem = pl.BlockSpec(memory_space=pltpu.SMEM)
-    codes = pl.BlockSpec((1, tokens, HD), lambda k, core: (0, 0, k))
-    block = (1, 2, half, HD)
+    codes = pl.BlockSpec((1, half, HD), lambda k, core: (0, core[0], k))
     return pl.pallas_call(
         prepare_kernel,
         grid_spec=pltpu.PrefetchScalarGridSpec(
             num_scalar_prefetch=1,
             grid=(KVH,),
-            in_specs=[smem, smem, codes, codes],
-            out_specs=[
-                pl.BlockSpec(block, lambda k, core: (core[0] * KVH + k, 0, 0, 0)),
-                pl.BlockSpec(block, lambda k, core: (k, 0, 0, 0)),
-            ],
+            in_specs=[smem] * 3
+            + [codes, codes, pl.BlockSpec((2, half, HD), lambda k, core: (0, 0, k))],
+            out_specs=pl.BlockSpec((2, 1, 2, half, HD), lambda k, core: (0, k, 0, 0, 0)),
         ),
-        out_shape=[
-            jax.ShapeDtypeStruct((2 * KVH, 2, half, HD), jnp.bfloat16),
-            jax.ShapeDtypeStruct((KVH, 2, half, HD), jnp.bfloat16),
-        ],
-        cost_estimate=pl.CostEstimate(flops=0, bytes_accessed=MIB // 8, transcendentals=0),
-    )(core, index, table, key_codes, value_codes)
+        out_shape=jax.ShapeDtypeStruct((2, KVH, 2, half, HD), jnp.bfloat16),
+        cost_estimate=pl.CostEstimate(flops=0, bytes_accessed=12 * MIB, transcendentals=0),
+    )(core, index, other_index, table, key_codes, value_codes, received)
 
 
 def attend_kernel(first, last, *refs):
@@ -286,7 +284,7 @@
             ],
             out_specs=[by_row(KVH, QROWS, HD)] * 2,
         ),
-        out_shape=[jax.ShapeDtypeStruct((rows, KVH, QROWS, HD), jnp.float32)] * 2,
+        out_shape=[pltpu.HBM((rows, KVH, QROWS, HD), jnp.float32)] * 2,
         compiler_params=pltpu.CompilerParams(vmem_limit_bytes=24 * MIB),
         cost_estimate=pl.CostEstimate(
             flops=4 * rows * QH * STEPS * suffix * HD,
@@ -361,10 +359,14 @@
     swap = [(i, i ^ 1) for i in range(groups)]
     names = row_prefix[:, 0]
 
+    half = prefix_key_codes.shape[1] // 2
+    sent = [
+        lax.dynamic_slice_in_dim(codes[0], (1 - core) * half, half, 0)
+        for codes in (prefix_key_codes, prefix_value_codes)
+    ]
+    received = lax.ppermute(jnp.stack(sent), "prefix", swap)
+    other_index = lax.ppermute(scale_index, "prefix", swap)
     outgoing, arranged = outgoing_queries(names, queries)
-    outgoing, key_codes, value_codes = lax.optimization_barrier(
-        (outgoing, prefix_key_codes, prefix_value_codes)
-    )
     arrived = lax.all_to_all(
         outgoing.reshape(groups * shards, QROWS, HD),
         ("prefix", "seq"),
@@ -372,12 +374,16 @@
         concat_axis=0,
         tiled=True,
     )
-    keep, send = prepare(
-        core.reshape(1).astype(jnp.int32), scale_index[0], scale_table, key_codes, value_codes
-    )
-    received = lax.ppermute(send, "prefix", swap)
     q = arrived.reshape(-1, HD)
-    moved = lax.dynamic_update_slice(keep, received, ((1 - core) * KVH, 0, 0, 0))
+    moved = prepare(
+        core.reshape(1).astype(jnp.int32),
+        scale_index[0],
+        other_index[0],
+        scale_table,
+        prefix_key_codes,
+        prefix_value_codes,
+        received,
+    ).reshape(2 * KVH, 2, half, HD)
     moved, q = lax.optimization_barrier((moved, q))
     own = lax.all_to_all(moved, "seq", split_axis=0, concat_axis=0, tiled=True)
     other = lax.ppermute(own, "prefix", swap)

time: 168 us -> 162 us (0.964)
  waiting for transfers between devices: 18.2 us -> 13.1 us
  local copies, waits for them, and re-layouts: 5.57 us -> 3.18 us
    all_to_all x1, waiting for transfers between devices: 17.8 us -> 10.3 us  [local(): lax.all_to_all(outgoing.reshape(groups * shards, QROWS, HD), ('prefix', '...]
    unnamed x15 -> x17, local copies, waits for them, and re-layouts: 4.32 us -> 1.69 us
  transfers between devices with their start and end apart: 4 -> 5, of which waited for: 2 -> 3; matrix products, arithmetic and copies ran while one was open for 1% -> 0% of each run, Pallas kernels for 26% -> 33%
where the time goes in v1:
time: 162 us; the launch traced here: 161 us
  Pallas kernels  85.3 us (53%)
  blocking collectives  42.7 us (26%)
  starting transfers between devices  16.8 us (10%)
  waiting for transfers between devices  13.1 us (8%)
  local copies, waits for them, and re-layouts  3.18 us (2%)
    pallas_call x2, Pallas kernels, attend(): pl.pallas_call(functools.partial(attend_kernel, first, last), in_specs=[v...  51.6 us
    all_to_all x1, blocking collectives, local(): own = lax.all_to_all(moved, 'seq', split_axis=0, concat_axis=0, tiled=True)  42.7 us
    pallas_call x1, Pallas kernels, local_attention(): pl.pallas_call(local_kernel, grid_spec=pltpu.PrefetchScalarGridSpec(num_s...  20.1 us
    all_to_all x1, starting transfers between devices, local(): lax.all_to_all(outgoing.reshape(groups * shards, QROWS, HD), ('prefix', '...  11.2 us
    all_to_all x1, waiting for transfers between devices, local(): lax.all_to_all(outgoing.reshape(groups * shards, QROWS, HD), ('prefix', '...  10.3 us
    pallas_call x1, Pallas kernels, prepare(): pl.pallas_call(prepare_kernel, grid_spec=pltpu.PrefetchScalarGridSpec(num...  6.88 us
    all_to_all x1, starting transfers between devices, local(): lax.all_to_all(answer, ('prefix', 'seq'), split_axis=0, concat_axis=0, ti...  5.39 us
    pallas_call x1, Pallas kernels, combine(): pl.pallas_call(combine_kernel, in_specs=[pl.BlockSpec(memory_space=pltpu....  4.19 us
  transfers between devices with their start and end apart: 5, of which 3 were waited for; matrix products, arithmetic and copies ran while one was open for 0% of the time, Pallas kernels for 33%

profile of v1, /device:TPU:0, one launch (start us, length us, event | category | flops | bytes accessed | tf_op | source)
XLA Modules:
  0.0 161.4 jit_solution(13758335115032189769)
XLA Ops:
  0.0 1.5 constant_dynamic-slice_fusion
  1.5 0.1 pad_maximum_fusion
  1.6 0.0 copy-start.7
  1.7 0.1 collective-permute-start.1
  1.8 2.5 %shard_map.110 = (bf16[16,8,32,128]{3,2,1,0:T(8,128)(2,1)}, bf16[8,8,32,128]{3,2,1,0:T(8,128)(2,1)}) custom-call(s32[8]{0:T(128)} %bitcast.17, bf16[8,4,8192]{2,1,0:T(4,128)(2,1)} %q_ref.1), custom_call_target="tpu_custom_call" | custom-call | bytes 2097152 | tf_op jit(solution)/shard_map/pallas_call | solution.py:68
  4.3 11.2 %all-to-all-start = ((bf16[128,32,128]{2,1,0:T(8,128)(2,1)}), bf16[128,32,128]{2,1,0:T(8,128)(2,1)S(1)}, u32[]{:S(2)}, u32[]{:S(2)}) async-start(bf16[128,32,128]{2,1,0:T(8,128)(2,1)} %bitcast.14), calls=%async_computation | async-start | bytes 2097152 | tf_op jit(solution)/shard_map/all_to_all | solution.py:370
  15.5 0.0 copy-done.7
  15.6 0.0 copy-start.5
  15.6 0.1 collective-permute-start
  15.7 1.2 collective-permute-done
  16.8 0.0 copy-start.6
  16.8 0.0 collective-permute-done.1.got_ref
  16.8 0.0 copy-done.5
  16.8 0.6 copy-done.6
  17.4 6.9 %shard_map.109 = bf16[2,8,2,384,128]{4,3,2,1,0:T(8,128)(2,1)} custom-call(s32[1]{0:T(128)} %bitcast.2.core_ref, s32[6,8]{1,0:T(8,128)} %bitcast.15, s32[6,8]{1,0:T(8,128)} %bitcast.16, f32[2,256]{1,0:T(2,128)} %table_ref.1, bf16[1,768,1024]{2,1,0:T(8,128)(2,1)} %k_ref.1, bf16[1,768,1024]{2,1,0:T(8,128)(2,1)} %v_ref.1, ...), custom_call_target="tpu_custom_call" | custom-call | bytes 12582912 | tf_op jit(solution)/shard_map/pallas_call | solution.py:108
  24.3 10.3 %all-to-all-done = bf16[128,32,128]{2,1,0:T(8,128)(2,1)S(1)} async-done(((bf16[128,32,128]{2,1,0:T(8,128)(2,1)}), bf16[128,32,128]{2,1,0:T(8,128)(2,1)S(1)}, u32[]{:S(2)}, u32[]{:S(2)}) %all-to-all-start) | async-done | bytes 1048608 | tf_op jit(solution)/shard_map/all_to_all | solution.py:370
  34.6 42.7 %all_to_all.15.refs_1_ = bf16[16,2,384,128]{3,2,1,0:T(8,128)(2,1)S(1)} all-to-all(bf16[16,2,384,128]{3,2,1,0:T(8,128)(2,1)} %bitcast.12), channel_id=1, replica_groups=mesh['prefix'=8,'seq'=16] {'seq'}, dimensions={0} | all-to-all | bytes 6291456 | tf_op jit(solution)/shard_map/all_to_all | solution.py:388
  77.3 0.0 collective-permute-start.2
  77.3 24.5 %shard_map.111.refs_2_ = f32[144,4096]{1,0:T(8,128)S(1)} custom-call(bf16[4096,128]{1,0:T(8,128)(2,1)S(1)} %bitcast.10, bf16[16,2,384,128]{3,2,1,0:T(8,128)(2,1)S(1)} %all_to_all.15.refs_1_), custom_call_target="tpu_custom_call" | custom-call | flops 25769803776 | bytes 4194304 | tf_op jit(solution)/shard_map/pallas_call | solution.py:226
  101.8 0.0 collective-permute-done.2.refs_1_
  101.8 27.1 %shard_map.112 = bf16[128,40,128]{2,1,0:T(8,128)(2,1)} custom-call(bf16[4096,128]{1,0:T(8,128)(2,1)S(1)} %bitcast.11, bf16[16,2,384,128]{3,2,1,0:T(8,128)(2,1)S(1)} %collective-permute-done.2.refs_1_, f32[144,4096]{1,0:T(8,128)S(1)} %shard_map.111.refs_2_), custom_call_target="tpu_custom_call" | custom-call | flops 25769803776 | bytes 4194304 | tf_op jit(solution)/shard_map/pallas_call | solution.py:226
  128.9 0.0 copy-start
  128.9 0.0 copy-start.1
  128.9 5.4 %all-to-all-start.2 = ((bf16[128,40,128]{2,1,0:T(8,128)(2,1)}), bf16[128,40,128]{2,1,0:T(8,128)(2,1)S(1)}, u32[]{:S(2)}, u32[]{:S(2)}) async-start(bf16[128,40,128]{2,1,0:T(8,128)(2,1)} %shard_map.112), calls=%async_computation.2 | async-start | bytes 2621440 | tf_op jit(solution)/shard_map/all_to_all | solution.py:395
  134.3 0.0 copy-done
  134.4 0.0 copy-done.1
  134.4 0.0 copy-done.2
  134.4 0.0 copy-done.3
  134.4 20.1 %shard_map.113 = (f32[8,8,32,128]{3,2,1,0:T(8,128)}, f32[8,8,32,128]{3,2,1,0:T(8,128)}) custom-call(s32[8]{0:T(128)S(1)} %copy-done.3, bf16[8,8,32,128]{3,2,1,0:T(8,128)(2,1)S(1)} %copy-done, bf16[8,4,1024]{2,1,0:T(4,128)(2,1)S(1)} %copy-done.1, bf16[8,4,1024]{2,1,0:T(4,128)(2,1)S(1)} %copy-done.2, bf16[8,256,1024]{2,1,0:T(8,128)(2,1)} %sk_ref.1, ...), custom_call_target="tpu_custom_call" | custom-call | flops 268435456 | bytes 10485760 | tf_op jit(solution)/shard_map/pallas_call | solution.py:273
  154.5 1.6 %all-to-all-done.2 = bf16[128,40,128]{2,1,0:T(8,128)(2,1)S(1)} async-done(((bf16[128,40,128]{2,1,0:T(8,128)(2,1)}), bf16[128,40,128]{2,1,0:T(8,128)(2,1)S(1)}, u32[]{:S(2)}, u32[]{:S(2)}) %all-to-all-start.2) | async-done | bytes 1310752 | tf_op jit(solution)/shard_map/all_to_all | solution.py:395
  156.1 1.1 copy-done.4
  157.2 4.2 %shard_map.114 = bf16[8,4,8192]{2,1,0:T(4,128)(2,1)} custom-call(s32[8]{0:T(128)} %bitcast.18, s32[1]{0:T(128)} %bitcast.1.first_lane, bf16[16,8,40,128]{3,2,1,0:T(8,128)(2,1)} %bitcast.13, f32[8,8,32,128]{3,2,1,0:T(8,128)} %get-tuple-element.15.out_ref, f32[8,8,32,128]{3,2,1,0:T(8,128)} %get-tuple-element.16.lse_ref), custom_call_target="tpu_custom_call" | custom-call | bytes 4194304 | tf_op jit(solution)/shard_map/pallas_call | solution.py:334
  (4 shorter events, 0.0 us)
Async XLA Ops:
  1.6 13.9 %copy-start.7 = (s32[1,6,8]{2,0,1:T(1,128)S(1)}, s32[1,6,8]{2,0,1:T(1,128)}, u32[]{:S(2)}) copy-start(s32[1,6,8]{2,0,1:T(1,128)} %param.20) | copy-start | bytes 580
  1.7 15.2 %collective-permute-start.1 = (bf16[2,384,1024]{2,1,0:T(8,128)(2,1)S(1)}, bf16[2,384,1024]{2,1,0:T(8,128)(2,1)}, u32[]{:S(2)}, u32[]{:S(2)}) collective-permute-start(bf16[2,384,1024]{2,1,0:T(8,128)(2,1)S(1)} %pad_maximum_fusion), channel_id=1, source_target_pairs={{0,16},{16,0},{32,48},{48,32},{64,80},{80,64},{96,112},{112,96},{1... | collective-permute-start | bytes 4718600 | tf_op jit(solution)/shard_map/ppermute | solution.py:367
  4.3 30.3 %all-to-all-start = ((bf16[128,32,128]{2,1,0:T(8,128)(2,1)}), bf16[128,32,128]{2,1,0:T(8,128)(2,1)S(1)}, u32[]{:S(2)}, u32[]{:S(2)}) async-start(bf16[128,32,128]{2,1,0:T(8,128)(2,1)} %bitcast.14), calls=%async_computation | async-start | bytes 2097152 | tf_op jit(solution)/shard_map/all_to_all | solution.py:370
  15.6 1.3 copy-start.5
  15.6 1.2 collective-permute-start
  16.8 0.6 copy-start.6
  77.3 24.5 %collective-permute-start.2 = (bf16[16,2,384,128]{3,2,1,0:T(8,128)(2,1)S(1)}, bf16[16,2,384,128]{3,2,1,0:T(8,128)(2,1)S(1)}, u32[]{:S(2)}, u32[]{:S(2)}) collective-permute-start(bf16[16,2,384,128]{3,2,1,0:T(8,128)(2,1)S(1)} %all_to_all.15.refs_1_), channel_id=1, source_target_pairs={{0,16},{16,0},{32,48},{48,32},{64,80},{80,64},{96,112},{112,96},{1... | collective-permute-start | bytes 9437192 | tf_op jit(solution)/shard_map/ppermute | solution.py:389
  128.9 5.4 %copy-start = (bf16[8,8,32,128]{3,2,1,0:T(8,128)(2,1)S(1)}, bf16[8,8,32,128]{3,2,1,0:T(8,128)(2,1)}, u32[]{:S(2)}) copy-start(bf16[8,8,32,128]{3,2,1,0:T(8,128)(2,1)} %get-tuple-element.14.q_ref) | copy-start | bytes 1572868
  128.9 5.4 %copy-start.1 = (bf16[8,4,1024]{2,1,0:T(4,128)(2,1)S(1)}, bf16[8,4,1024]{2,1,0:T(4,128)(2,1)}, u32[]{:S(2)}) copy-start(bf16[8,4,1024]{2,1,0:T(4,128)(2,1)} %nk_ref.1) | copy-start | bytes 196612
  128.9 5.4 %copy-start.2 = (bf16[8,4,1024]{2,1,0:T(4,128)(2,1)S(1)}, bf16[8,4,1024]{2,1,0:T(4,128)(2,1)}, u32[]{:S(2)}) copy-start(bf16[8,4,1024]{2,1,0:T(4,128)(2,1)} %nv_ref.1) | copy-start | bytes 196612
  128.9 5.4 %copy-start.3 = (s32[8]{0:T(128)S(1)}, s32[8]{0:T(128)}, u32[]{:S(2)}) copy-start(s32[8]{0:T(128)} %lens.1) | copy-start | bytes 100
  128.9 27.2 %all-to-all-start.2 = ((bf16[128,40,128]{2,1,0:T(8,128)(2,1)}), bf16[128,40,128]{2,1,0:T(8,128)(2,1)S(1)}, u32[]{:S(2)}, u32[]{:S(2)}) async-start(bf16[128,40,128]{2,1,0:T(8,128)(2,1)} %shard_map.112), calls=%async_computation.2 | async-start | bytes 2621440 | tf_op jit(solution)/shard_map/all_to_all | solution.py:395
  156.1 1.1 copy-start.4

commit v2 on v1

--- a/solution.py
+++ b/solution.py
@@ -336,8 +336,9 @@
         in_specs=[pl.BlockSpec(memory_space=pltpu.SMEM)] * 2 + [vmem] * 3,
         out_specs=vmem,
         out_shape=jax.ShapeDtypeStruct((rows, STEPS, QH * HD), jnp.bfloat16),
+        compiler_params=pltpu.CompilerParams(vmem_limit_bytes=16 * MIB),
         cost_estimate=pl.CostEstimate(flops=0, bytes_accessed=4 * MIB, transcendentals=0),
-    )(names, first_lane, in_hbm(back), in_hbm(local_out), in_hbm(local_lse))
+    )(names, first_lane, back, in_hbm(local_out), in_hbm(local_lse))
 
 
 def local(

time: 162 us -> 160 us (0.988)
  transfers between devices with their start and end apart: 5 -> 5, of which waited for: 3 -> 3; matrix products, arithmetic and copies ran while one was open for 0% -> 0% of each run, Pallas kernels for 33% -> 34%
where the time goes in v2:
time: 160 us
  Pallas kernels  84.9 us (53%)
  blocking collectives  42.7 us (27%)
  starting transfers between devices  16.8 us (10%)
  waiting for transfers between devices  13.1 us (8%)
  local copies, waits for them, and re-layouts  2.11 us (1%)
    pallas_call x2, Pallas kernels, attend(): pl.pallas_call(functools.partial(attend_kernel, first, last), in_specs=[v...  51.6 us
    all_to_all x1, blocking collectives, local(): own = lax.all_to_all(moved, 'seq', split_axis=0, concat_axis=0, tiled=True)  42.7 us
    pallas_call x1, Pallas kernels, local_attention(): pl.pallas_call(local_kernel, grid_spec=pltpu.PrefetchScalarGridSpec(num_s...  20.1 us
    all_to_all x1, starting transfers between devices, local(): lax.all_to_all(outgoing.reshape(groups * shards, QROWS, HD), ('prefix', '...  11.2 us
    all_to_all x1, waiting for transfers between devices, local(): lax.all_to_all(outgoing.reshape(groups * shards, QROWS, HD), ('prefix', '...  10.3 us
    pallas_call x1, Pallas kernels, prepare(): pl.pallas_call(prepare_kernel, grid_spec=pltpu.PrefetchScalarGridSpec(num...  6.88 us
    all_to_all x1, starting transfers between devices, local(): lax.all_to_all(answer, ('prefix', 'seq'), split_axis=0, concat_axis=0, ti...  5.39 us
    pallas_call x1, Pallas kernels, combine(): pl.pallas_call(combine_kernel, in_specs=[pl.BlockSpec(memory_space=pltpu....  3.8 us
  transfers between devices with their start and end apart: 5, of which 3 were waited for; matrix products, arithmetic and copies ran while one was open for 0% of the time, Pallas kernels for 34%

profile of v2, /device:TPU:0, one launch (start us, length us, event | category | flops | bytes accessed | tf_op | source)
XLA Modules:
  0.0 159.9 jit_solution(245391556926625038)
XLA Ops:
  0.0 1.5 constant_dynamic-slice_fusion
  1.5 0.1 pad_maximum_fusion
  1.6 0.0 copy-start.7
  1.7 0.1 collective-permute-start.1
  1.8 2.5 %shard_map.110 = (bf16[16,8,32,128]{3,2,1,0:T(8,128)(2,1)}, bf16[8,8,32,128]{3,2,1,0:T(8,128)(2,1)}) custom-call(s32[8]{0:T(128)} %bitcast.13, bf16[8,4,8192]{2,1,0:T(4,128)(2,1)} %q_ref.1), custom_call_target="tpu_custom_call" | custom-call | bytes 2097152 | tf_op jit(solution)/shard_map/pallas_call | solution.py:68
  4.3 11.2 %all-to-all-start = ((bf16[128,32,128]{2,1,0:T(8,128)(2,1)}), bf16[128,32,128]{2,1,0:T(8,128)(2,1)S(1)}, u32[]{:S(2)}, u32[]{:S(2)}) async-start(bf16[128,32,128]{2,1,0:T(8,128)(2,1)} %bitcast.16), calls=%async_computation | async-start | bytes 2097152 | tf_op jit(solution)/shard_map/all_to_all | solution.py:371
  15.5 0.0 copy-done.7
  15.6 0.0 copy-start.5
  15.6 0.1 collective-permute-start
  15.7 1.2 collective-permute-done
  16.8 0.0 copy-start.6
  16.8 0.0 collective-permute-done.1.got_ref
  16.8 0.0 copy-done.5
  16.8 0.6 copy-done.6
  17.4 6.9 %shard_map.109 = bf16[2,8,2,384,128]{4,3,2,1,0:T(8,128)(2,1)} custom-call(s32[1]{0:T(128)} %bitcast.2.core_ref, s32[6,8]{1,0:T(8,128)} %bitcast.17, s32[6,8]{1,0:T(8,128)} %bitcast.18, f32[2,256]{1,0:T(2,128)} %table_ref.1, bf16[1,768,1024]{2,1,0:T(8,128)(2,1)} %k_ref.1, bf16[1,768,1024]{2,1,0:T(8,128)(2,1)} %v_ref.1, ...), custom_call_target="tpu_custom_call" | custom-call | bytes 12582912 | tf_op jit(solution)/shard_map/pallas_call | solution.py:108
  24.3 10.3 %all-to-all-done = bf16[128,32,128]{2,1,0:T(8,128)(2,1)S(1)} async-done(((bf16[128,32,128]{2,1,0:T(8,128)(2,1)}), bf16[128,32,128]{2,1,0:T(8,128)(2,1)S(1)}, u32[]{:S(2)}, u32[]{:S(2)}) %all-to-all-start) | async-done | bytes 1048608 | tf_op jit(solution)/shard_map/all_to_all | solution.py:371
  34.6 42.7 %all_to_all.15.refs_1_ = bf16[16,2,384,128]{3,2,1,0:T(8,128)(2,1)S(1)} all-to-all(bf16[16,2,384,128]{3,2,1,0:T(8,128)(2,1)} %bitcast.15), channel_id=1, replica_groups=mesh['prefix'=8,'seq'=16] {'seq'}, dimensions={0} | all-to-all | bytes 6291456 | tf_op jit(solution)/shard_map/all_to_all | solution.py:389
  77.3 0.0 collective-permute-start.2
  77.3 24.5 %shard_map.111.refs_2_ = f32[144,4096]{1,0:T(8,128)S(1)} custom-call(bf16[4096,128]{1,0:T(8,128)(2,1)S(1)} %bitcast.11, bf16[16,2,384,128]{3,2,1,0:T(8,128)(2,1)S(1)} %all_to_all.15.refs_1_), custom_call_target="tpu_custom_call" | custom-call | flops 25769803776 | bytes 4194304 | tf_op jit(solution)/shard_map/pallas_call | solution.py:226
  101.8 0.0 collective-permute-done.2.refs_1_
  101.8 27.1 %shard_map.112 = bf16[128,40,128]{2,1,0:T(8,128)(2,1)} custom-call(bf16[4096,128]{1,0:T(8,128)(2,1)S(1)} %bitcast.12, bf16[16,2,384,128]{3,2,1,0:T(8,128)(2,1)S(1)} %collective-permute-done.2.refs_1_, f32[144,4096]{1,0:T(8,128)S(1)} %shard_map.111.refs_2_), custom_call_target="tpu_custom_call" | custom-call | flops 25769803776 | bytes 4194304 | tf_op jit(solution)/shard_map/pallas_call | solution.py:226
  128.9 0.0 copy-start
  128.9 5.4 %all-to-all-start.2 = ((bf16[128,40,128]{2,1,0:T(8,128)(2,1)}), bf16[128,40,128]{2,1,0:T(8,128)(2,1)S(1)}, u32[]{:S(2)}, u32[]{:S(2)}) async-start(bf16[128,40,128]{2,1,0:T(8,128)(2,1)} %shard_map.112), calls=%async_computation.2 | async-start | bytes 2621440 | tf_op jit(solution)/shard_map/all_to_all | solution.py:396
  134.3 0.0 copy-done
  134.4 0.0 copy-done.1
  134.4 0.0 copy-done.2
  134.4 0.0 copy-done.4
  134.4 0.0 copy-start.3
  134.4 20.1 %shard_map.113 = (f32[8,8,32,128]{3,2,1,0:T(8,128)}, f32[8,8,32,128]{3,2,1,0:T(8,128)}) custom-call(s32[8]{0:T(128)S(1)} %copy-done.4, bf16[8,8,32,128]{3,2,1,0:T(8,128)(2,1)S(1)} %copy-done, bf16[8,4,1024]{2,1,0:T(4,128)(2,1)S(1)} %copy-done.1, bf16[8,4,1024]{2,1,0:T(4,128)(2,1)S(1)} %copy-done.2, bf16[8,256,1024]{2,1,0:T(8,128)(2,1)} %sk_ref.1, ...), custom_call_target="tpu_custom_call" | custom-call | flops 268435456 | bytes 10485760 | tf_op jit(solution)/shard_map/pallas_call | solution.py:273
  154.5 1.6 %all-to-all-done.2 = bf16[128,40,128]{2,1,0:T(8,128)(2,1)S(1)} async-done(((bf16[128,40,128]{2,1,0:T(8,128)(2,1)}), bf16[128,40,128]{2,1,0:T(8,128)(2,1)S(1)}, u32[]{:S(2)}, u32[]{:S(2)}) %all-to-all-start.2) | async-done | bytes 1310752 | tf_op jit(solution)/shard_map/all_to_all | solution.py:396
  156.1 0.0 copy-done.3
  156.1 3.8 %shard_map.114 = bf16[8,4,8192]{2,1,0:T(4,128)(2,1)} custom-call(s32[8]{0:T(128)S(1)} %bitcast.14, s32[1]{0:T(128)} %bitcast.1.first_lane, bf16[16,8,40,128]{3,2,1,0:T(8,128)(2,1)S(1)} %bitcast.10, f32[8,8,32,128]{3,2,1,0:T(8,128)} %get-tuple-element.15.out_ref, f32[8,8,32,128]{3,2,1,0:T(8,128)} %get-tuple-element.16.lse_ref), custom_call_target="tpu_custom_call" | custom-call | bytes 4194304 | tf_op jit(solution)/shard_map/pallas_call | solution.py:334
  (4 shorter events, 0.0 us)
Async XLA Ops:
  1.6 13.9 %copy-start.7 = (s32[1,6,8]{2,0,1:T(1,128)S(1)}, s32[1,6,8]{2,0,1:T(1,128)}, u32[]{:S(2)}) copy-start(s32[1,6,8]{2,0,1:T(1,128)} %param.20) | copy-start | bytes 580
  1.7 15.2 %collective-permute-start.1 = (bf16[2,384,1024]{2,1,0:T(8,128)(2,1)S(1)}, bf16[2,384,1024]{2,1,0:T(8,128)(2,1)}, u32[]{:S(2)}, u32[]{:S(2)}) collective-permute-start(bf16[2,384,1024]{2,1,0:T(8,128)(2,1)S(1)} %pad_maximum_fusion), channel_id=1, source_target_pairs={{0,16},{16,0},{32,48},{48,32},{64,80},{80,64},{96,112},{112,96},{1... | collective-permute-start | bytes 4718600 | tf_op jit(solution)/shard_map/ppermute | solution.py:368
  4.3 30.3 %all-to-all-start = ((bf16[128,32,128]{2,1,0:T(8,128)(2,1)}), bf16[128,32,128]{2,1,0:T(8,128)(2,1)S(1)}, u32[]{:S(2)}, u32[]{:S(2)}) async-start(bf16[128,32,128]{2,1,0:T(8,128)(2,1)} %bitcast.16), calls=%async_computation | async-start | bytes 2097152 | tf_op jit(solution)/shard_map/all_to_all | solution.py:371
  15.6 1.3 copy-start.5
  15.6 1.2 collective-permute-start
  16.8 0.6 copy-start.6
  77.3 24.5 %collective-permute-start.2 = (bf16[16,2,384,128]{3,2,1,0:T(8,128)(2,1)S(1)}, bf16[16,2,384,128]{3,2,1,0:T(8,128)(2,1)S(1)}, u32[]{:S(2)}, u32[]{:S(2)}) collective-permute-start(bf16[16,2,384,128]{3,2,1,0:T(8,128)(2,1)S(1)} %all_to_all.15.refs_1_), channel_id=1, source_target_pairs={{0,16},{16,0},{32,48},{48,32},{64,80},{80,64},{96,112},{112,96},{1... | collective-permute-start | bytes 9437192 | tf_op jit(solution)/shard_map/ppermute | solution.py:390
  128.9 5.4 %copy-start = (bf16[8,8,32,128]{3,2,1,0:T(8,128)(2,1)S(1)}, bf16[8,8,32,128]{3,2,1,0:T(8,128)(2,1)}, u32[]{:S(2)}) copy-start(bf16[8,8,32,128]{3,2,1,0:T(8,128)(2,1)} %get-tuple-element.14.q_ref) | copy-start | bytes 1572868
  128.9 5.4 %copy-start.1 = (bf16[8,4,1024]{2,1,0:T(4,128)(2,1)S(1)}, bf16[8,4,1024]{2,1,0:T(4,128)(2,1)}, u32[]{:S(2)}) copy-start(bf16[8,4,1024]{2,1,0:T(4,128)(2,1)} %nk_ref.1) | copy-start | bytes 196612
  128.9 5.4 %copy-start.2 = (bf16[8,4,1024]{2,1,0:T(4,128)(2,1)S(1)}, bf16[8,4,1024]{2,1,0:T(4,128)(2,1)}, u32[]{:S(2)}) copy-start(bf16[8,4,1024]{2,1,0:T(4,128)(2,1)} %nv_ref.1) | copy-start | bytes 196612
  128.9 5.4 %copy-start.4 = (s32[8]{0:T(128)S(1)}, s32[8]{0:T(128)}, u32[]{:S(2)}) copy-start(s32[8]{0:T(128)} %lens.1) | copy-start | bytes 100
  128.9 27.2 %all-to-all-start.2 = ((bf16[128,40,128]{2,1,0:T(8,128)(2,1)}), bf16[128,40,128]{2,1,0:T(8,128)(2,1)S(1)}, u32[]{:S(2)}, u32[]{:S(2)}) async-start(bf16[128,40,128]{2,1,0:T(8,128)(2,1)} %shard_map.112), calls=%async_computation.2 | async-start | bytes 2621440 | tf_op jit(solution)/shard_map/all_to_all | solution.py:396
  134.4 21.7 %copy-start.3 = (s32[8,1]{0,1:T(1,128)S(1)}, s32[8,1]{0,1:T(1,128)}, u32[]{:S(2)}) copy-start(s32[8,1]{0,1:T(1,128)} %param.17) | copy-start | bytes 100

commit v3 on v2

--- a/solution.py
+++ b/solution.py
@@ -321,7 +321,7 @@
                 ].astype(jnp.bfloat16)
         return carry
 
-    lax.fori_loop(0, rows, mix, 0)
+    lax.fori_loop(0, rows, mix, 0, unroll=2)
 
 
 def in_hbm(x):

time: 160 us -> 160 us (level)
  no operation moved by 1% of the time
where the time goes in v3:
time: 160 us; the launch traced here: 159 us
  Pallas kernels  84.5 us (53%)
  blocking collectives  42.7 us (27%)
  starting transfers between devices  16.8 us (10%)
  waiting for transfers between devices  13.1 us (8%)
  local copies, waits for them, and re-layouts  2.11 us (1%)
    pallas_call x2, Pallas kernels, attend(): pl.pallas_call(functools.partial(attend_kernel, first, last), in_specs=[v...  51.6 us
    all_to_all x1, blocking collectives, local(): own = lax.all_to_all(moved, 'seq', split_axis=0, concat_axis=0, tiled=True)  42.7 us
    pallas_call x1, Pallas kernels, local_attention(): pl.pallas_call(local_kernel, grid_spec=pltpu.PrefetchScalarGridSpec(num_s...  20.1 us
    all_to_all x1, starting transfers between devices, local(): lax.all_to_all(outgoing.reshape(groups * shards, QROWS, HD), ('prefix', '...  11.2 us
    all_to_all x1, waiting for transfers between devices, local(): lax.all_to_all(outgoing.reshape(groups * shards, QROWS, HD), ('prefix', '...  10.3 us
    pallas_call x1, Pallas kernels, prepare(): pl.pallas_call(prepare_kernel, grid_spec=pltpu.PrefetchScalarGridSpec(num...  6.88 us
    all_to_all x1, starting transfers between devices, local(): lax.all_to_all(answer, ('prefix', 'seq'), split_axis=0, concat_axis=0, ti...  5.39 us
    pallas_call x1, Pallas kernels, combine(): pl.pallas_call(combine_kernel, in_specs=[pl.BlockSpec(memory_space=pltpu....  3.37 us
  transfers between devices with their start and end apart: 5, of which 3 were waited for; matrix products, arithmetic and copies ran while one was open for 0% of the time, Pallas kernels for 34%

profile of v3, /device:TPU:0, one launch (start us, length us, event | category | flops | bytes accessed | tf_op | source)
XLA Modules:
  0.0 159.5 jit_solution(2637958061968591598)
XLA Ops:
  0.0 1.5 constant_dynamic-slice_fusion
  1.5 0.1 pad_maximum_fusion
  1.6 0.0 copy-start.7
  1.7 0.1 collective-permute-start.1
  1.8 2.5 %shard_map.110 = (bf16[16,8,32,128]{3,2,1,0:T(8,128)(2,1)}, bf16[8,8,32,128]{3,2,1,0:T(8,128)(2,1)}) custom-call(s32[8]{0:T(128)} %bitcast.13, bf16[8,4,8192]{2,1,0:T(4,128)(2,1)} %q_ref.1), custom_call_target="tpu_custom_call" | custom-call | bytes 2097152 | tf_op jit(solution)/shard_map/pallas_call | solution.py:68
  4.3 11.2 %all-to-all-start = ((bf16[128,32,128]{2,1,0:T(8,128)(2,1)}), bf16[128,32,128]{2,1,0:T(8,128)(2,1)S(1)}, u32[]{:S(2)}, u32[]{:S(2)}) async-start(bf16[128,32,128]{2,1,0:T(8,128)(2,1)} %bitcast.16), calls=%async_computation | async-start | bytes 2097152 | tf_op jit(solution)/shard_map/all_to_all | solution.py:371
  15.5 0.0 copy-done.7
  15.6 0.0 copy-start.5
  15.6 0.1 collective-permute-start
  15.7 1.2 collective-permute-done
  16.8 0.0 copy-start.6
  16.8 0.0 collective-permute-done.1.got_ref
  16.8 0.0 copy-done.5
  16.8 0.6 copy-done.6
  17.4 6.9 %shard_map.109 = bf16[2,8,2,384,128]{4,3,2,1,0:T(8,128)(2,1)} custom-call(s32[1]{0:T(128)} %bitcast.2.core_ref, s32[6,8]{1,0:T(8,128)} %bitcast.17, s32[6,8]{1,0:T(8,128)} %bitcast.18, f32[2,256]{1,0:T(2,128)} %table_ref.1, bf16[1,768,1024]{2,1,0:T(8,128)(2,1)} %k_ref.1, bf16[1,768,1024]{2,1,0:T(8,128)(2,1)} %v_ref.1, ...), custom_call_target="tpu_custom_call" | custom-call | bytes 12582912 | tf_op jit(solution)/shard_map/pallas_call | solution.py:108
  24.3 10.3 %all-to-all-done = bf16[128,32,128]{2,1,0:T(8,128)(2,1)S(1)} async-done(((bf16[128,32,128]{2,1,0:T(8,128)(2,1)}), bf16[128,32,128]{2,1,0:T(8,128)(2,1)S(1)}, u32[]{:S(2)}, u32[]{:S(2)}) %all-to-all-start) | async-done | bytes 1048608 | tf_op jit(solution)/shard_map/all_to_all | solution.py:371
  34.6 42.7 %all_to_all.15.refs_1_ = bf16[16,2,384,128]{3,2,1,0:T(8,128)(2,1)S(1)} all-to-all(bf16[16,2,384,128]{3,2,1,0:T(8,128)(2,1)} %bitcast.15), channel_id=1, replica_groups=mesh['prefix'=8,'seq'=16] {'seq'}, dimensions={0} | all-to-all | bytes 6291456 | tf_op jit(solution)/shard_map/all_to_all | solution.py:389
  77.3 0.0 collective-permute-start.2
  77.3 24.5 %shard_map.111.refs_2_ = f32[144,4096]{1,0:T(8,128)S(1)} custom-call(bf16[4096,128]{1,0:T(8,128)(2,1)S(1)} %bitcast.11, bf16[16,2,384,128]{3,2,1,0:T(8,128)(2,1)S(1)} %all_to_all.15.refs_1_), custom_call_target="tpu_custom_call" | custom-call | flops 25769803776 | bytes 4194304 | tf_op jit(solution)/shard_map/pallas_call | solution.py:226
  101.8 0.0 collective-permute-done.2.refs_1_
  101.8 27.1 %shard_map.112 = bf16[128,40,128]{2,1,0:T(8,128)(2,1)} custom-call(bf16[4096,128]{1,0:T(8,128)(2,1)S(1)} %bitcast.12, bf16[16,2,384,128]{3,2,1,0:T(8,128)(2,1)S(1)} %collective-permute-done.2.refs_1_, f32[144,4096]{1,0:T(8,128)S(1)} %shard_map.111.refs_2_), custom_call_target="tpu_custom_call" | custom-call | flops 25769803776 | bytes 4194304 | tf_op jit(solution)/shard_map/pallas_call | solution.py:226
  128.9 0.0 copy-start
  128.9 5.4 %all-to-all-start.2 = ((bf16[128,40,128]{2,1,0:T(8,128)(2,1)}), bf16[128,40,128]{2,1,0:T(8,128)(2,1)S(1)}, u32[]{:S(2)}, u32[]{:S(2)}) async-start(bf16[128,40,128]{2,1,0:T(8,128)(2,1)} %shard_map.112), calls=%async_computation.2 | async-start | bytes 2621440 | tf_op jit(solution)/shard_map/all_to_all | solution.py:396
  134.3 0.0 copy-done
  134.4 0.0 copy-done.1
  134.4 0.0 copy-done.2
  134.4 0.0 copy-done.4
  134.4 0.0 copy-start.3
  134.4 20.1 %shard_map.113 = (f32[8,8,32,128]{3,2,1,0:T(8,128)}, f32[8,8,32,128]{3,2,1,0:T(8,128)}) custom-call(s32[8]{0:T(128)S(1)} %copy-done.4, bf16[8,8,32,128]{3,2,1,0:T(8,128)(2,1)S(1)} %copy-done, bf16[8,4,1024]{2,1,0:T(4,128)(2,1)S(1)} %copy-done.1, bf16[8,4,1024]{2,1,0:T(4,128)(2,1)S(1)} %copy-done.2, bf16[8,256,1024]{2,1,0:T(8,128)(2,1)} %sk_ref.1, ...), custom_call_target="tpu_custom_call" | custom-call | flops 268435456 | bytes 10485760 | tf_op jit(solution)/shard_map/pallas_call | solution.py:273
  154.5 1.6 %all-to-all-done.2 = bf16[128,40,128]{2,1,0:T(8,128)(2,1)S(1)} async-done(((bf16[128,40,128]{2,1,0:T(8,128)(2,1)}), bf16[128,40,128]{2,1,0:T(8,128)(2,1)S(1)}, u32[]{:S(2)}, u32[]{:S(2)}) %all-to-all-start.2) | async-done | bytes 1310752 | tf_op jit(solution)/shard_map/all_to_all | solution.py:396
  156.1 0.0 copy-done.3
  156.1 3.4 %shard_map.114 = bf16[8,4,8192]{2,1,0:T(4,128)(2,1)} custom-call(s32[8]{0:T(128)S(1)} %bitcast.14, s32[1]{0:T(128)} %bitcast.1.first_lane, bf16[16,8,40,128]{3,2,1,0:T(8,128)(2,1)S(1)} %bitcast.10, f32[8,8,32,128]{3,2,1,0:T(8,128)} %get-tuple-element.15.out_ref, f32[8,8,32,128]{3,2,1,0:T(8,128)} %get-tuple-element.16.lse_ref), custom_call_target="tpu_custom_call" | custom-call | bytes 4194304 | tf_op jit(solution)/shard_map/pallas_call | solution.py:334
  (4 shorter events, 0.0 us)
Async XLA Ops:
  1.6 13.9 %copy-start.7 = (s32[1,6,8]{2,0,1:T(1,128)S(1)}, s32[1,6,8]{2,0,1:T(1,128)}, u32[]{:S(2)}) copy-start(s32[1,6,8]{2,0,1:T(1,128)} %param.20) | copy-start | bytes 580
  1.7 15.2 %collective-permute-start.1 = (bf16[2,384,1024]{2,1,0:T(8,128)(2,1)S(1)}, bf16[2,384,1024]{2,1,0:T(8,128)(2,1)}, u32[]{:S(2)}, u32[]{:S(2)}) collective-permute-start(bf16[2,384,1024]{2,1,0:T(8,128)(2,1)S(1)} %pad_maximum_fusion), channel_id=1, source_target_pairs={{0,16},{16,0},{32,48},{48,32},{64,80},{80,64},{96,112},{112,96},{1... | collective-permute-start | bytes 4718600 | tf_op jit(solution)/shard_map/ppermute | solution.py:368
  4.3 30.3 %all-to-all-start = ((bf16[128,32,128]{2,1,0:T(8,128)(2,1)}), bf16[128,32,128]{2,1,0:T(8,128)(2,1)S(1)}, u32[]{:S(2)}, u32[]{:S(2)}) async-start(bf16[128,32,128]{2,1,0:T(8,128)(2,1)} %bitcast.16), calls=%async_computation | async-start | bytes 2097152 | tf_op jit(solution)/shard_map/all_to_all | solution.py:371
  15.6 1.3 copy-start.5
  15.6 1.2 collective-permute-start
  16.8 0.6 copy-start.6
  77.3 24.5 %collective-permute-start.2 = (bf16[16,2,384,128]{3,2,1,0:T(8,128)(2,1)S(1)}, bf16[16,2,384,128]{3,2,1,0:T(8,128)(2,1)S(1)}, u32[]{:S(2)}, u32[]{:S(2)}) collective-permute-start(bf16[16,2,384,128]{3,2,1,0:T(8,128)(2,1)S(1)} %all_to_all.15.refs_1_), channel_id=1, source_target_pairs={{0,16},{16,0},{32,48},{48,32},{64,80},{80,64},{96,112},{112,96},{1... | collective-permute-start | bytes 9437192 | tf_op jit(solution)/shard_map/ppermute | solution.py:390
  128.9 5.4 %copy-start = (bf16[8,8,32,128]{3,2,1,0:T(8,128)(2,1)S(1)}, bf16[8,8,32,128]{3,2,1,0:T(8,128)(2,1)}, u32[]{:S(2)}) copy-start(bf16[8,8,32,128]{3,2,1,0:T(8,128)(2,1)} %get-tuple-element.14.q_ref) | copy-start | bytes 1572868
  128.9 5.4 %copy-start.1 = (bf16[8,4,1024]{2,1,0:T(4,128)(2,1)S(1)}, bf16[8,4,1024]{2,1,0:T(4,128)(2,1)}, u32[]{:S(2)}) copy-start(bf16[8,4,1024]{2,1,0:T(4,128)(2,1)} %nk_ref.1) | copy-start | bytes 196612
  128.9 5.4 %copy-start.2 = (bf16[8,4,1024]{2,1,0:T(4,128)(2,1)S(1)}, bf16[8,4,1024]{2,1,0:T(4,128)(2,1)}, u32[]{:S(2)}) copy-start(bf16[8,4,1024]{2,1,0:T(4,128)(2,1)} %nv_ref.1) | copy-start | bytes 196612
  128.9 5.4 %copy-start.4 = (s32[8]{0:T(128)S(1)}, s32[8]{0:T(128)}, u32[]{:S(2)}) copy-start(s32[8]{0:T(128)} %lens.1) | copy-start | bytes 100
  128.9 27.2 %all-to-all-start.2 = ((bf16[128,40,128]{2,1,0:T(8,128)(2,1)}), bf16[128,40,128]{2,1,0:T(8,128)(2,1)S(1)}, u32[]{:S(2)}, u32[]{:S(2)}) async-start(bf16[128,40,128]{2,1,0:T(8,128)(2,1)} %shard_map.112), calls=%async_computation.2 | async-start | bytes 2621440 | tf_op jit(solution)/shard_map/all_to_all | solution.py:396
  134.4 21.7 %copy-start.3 = (s32[8,1]{0,1:T(1,128)S(1)}, s32[8,1]{0,1:T(1,128)}, u32[]{:S(2)}) copy-start(s32[8,1]{0,1:T(1,128)} %param.17) | copy-start | bytes 100
